TPU v7x, 128 devices: a whole 4x4x4 slice. The times are simulated.
128 devices in a mesh: fsdp: 32 (over z, x, core), feat: 4 (over y).
Axes of the slice: x: 4, y: 4, z: 4, core: 2. Of those that a mesh axis runs over, the one named last changes fastest.
Arguments:
- table_cells: bfloat16 [1536, 256, 192], P(('fsdp', 'feat'))
- attn_weights: bfloat16 [8, 192, 192], P(None, 'fsdp')
- hidden_up_weight: bfloat16 [192, 384], P('fsdp'), may hold values from -0.4375 to 0.4375
- hidden_down_weight: bfloat16 [384, 192], P('fsdp'), may hold values from -0.3125 to 0.3125
- norm_gains: float32 [3, 192], replicated, may hold values from 0.25 to 1.75
- train_count: int32 [1], replicated, may hold values from 384 to 1152
- feature_count: int32 [1], replicated, may hold values from 128 to 256
Outputs:
- layer_out: bfloat16 [1536, 256, 192], P(('fsdp', 'feat'))
Inputs may be any that keep to these rules, and one draw needn't show every extreme that they name: Rows 0 to train_count - 1 are the training rows. Features 0 to feature_count - 1 are real, the others padding.
All inputs are finite; a program needn't handle non-finite values.
Results may differ from a plain program's by a relative error of at most 0.012.
The roundings to bfloat16 on the way count: a program that leaves them out, or rounds other values in their place, can miss the bound.
Values may be sent and summed in bfloat16 or wider, within the bound.
A program may use at most 128 MiB of HBM per device.

v0:
```python
import jax
import jax.numpy as jnp
from jax import lax
from jax.sharding import PartitionSpec as P

HEADS = 6
EPS = 1e-05
NEGATIVE = -1e30


def normalize(value_rows, gain):
    floats = value_rows.astype(jnp.float32)
    average = jnp.mean(floats, axis=-1, keepdims=True)
    centered = floats - average
    variance = jnp.mean(centered * centered, axis=-1, keepdims=True)
    return (centered * lax.rsqrt(variance + EPS) * gain).astype(jnp.bfloat16)


def softmax_rows(scores, live):
    masked = jnp.where(live, scores, NEGATIVE)
    row_maximum = jnp.max(masked, axis=-1, keepdims=True)
    exponent = jnp.exp(masked - row_maximum)
    return (exponent / jnp.sum(exponent, axis=-1, keepdims=True)).astype(jnp.bfloat16)


def project(normed, weight):
    model_width = normed.shape[-1]
    product = jnp.dot(normed.reshape(-1, model_width), weight, preferred_element_type=jnp.float32)
    return product.astype(jnp.bfloat16).reshape(normed.shape[:-1] + (weight.shape[1],))


def output_proj(attended_rows, residual, weight):
    model_width = attended_rows.shape[-1]
    product = jnp.dot(
        attended_rows.reshape(-1, model_width), weight, preferred_element_type=jnp.float32
    )
    return (residual.astype(jnp.float32) + product.reshape(residual.shape)).astype(jnp.bfloat16)


def feature_attention(table_cells, normed, weights, feat_live):
    model_width = normed.shape[-1]
    head_size = model_width // HEADS
    queries = project(normed, weights[0])
    keys = project(normed, weights[1])
    value_rows = project(normed, weights[2])
    outputs = []
    for index_head in range(HEADS):
        training_extent = slice(index_head * head_size, (index_head + 1) * head_size)
        scores = jnp.einsum(
            "rqe,rke->rqk",
            queries[..., training_extent],
            keys[..., training_extent],
            preferred_element_type=jnp.float32,
        ) * head_size ** (-0.5)
        attention_probabilities = softmax_rows(scores, feat_live[None, None, :])
        outputs.append(
            jnp.einsum(
                "rqk,rke->rqe",
                attention_probabilities,
                value_rows[..., training_extent],
                preferred_element_type=jnp.float32,
            ).astype(jnp.bfloat16)
        )
    return output_proj(jnp.concatenate(outputs, axis=-1), table_cells, weights[3])


def sample_attention(column_block, normed, weights, row_live):
    all_rows, feat_here, model_width = normed.shape
    head_size = model_width // HEADS
    queries = project(normed, weights[4])
    keys = project(normed, weights[5])
    value_rows = project(normed, weights[6])
    block_count = max(1, all_rows // 512)
    block_rows = all_rows // block_count
    query_blocks = queries.reshape(block_count, block_rows, feat_here, model_width)

    def one_block(query_block):
        outputs = []
        for index_head in range(HEADS):
            training_extent = slice(index_head * head_size, (index_head + 1) * head_size)
            scores = jnp.einsum(
                "vsg,psg->svp",
                query_block[..., training_extent],
                keys[..., training_extent],
                preferred_element_type=jnp.float32,
            ) * head_size ** (-0.5)
            attention_probabilities = softmax_rows(scores, row_live[None, None, :])
            outputs.append(
                jnp.einsum(
                    "tdj,jtn->dtn",
                    attention_probabilities,
                    value_rows[..., training_extent],
                    preferred_element_type=jnp.float32,
                ).astype(jnp.bfloat16)
            )
        return jnp.concatenate(outputs, axis=-1)

    attended_rows = lax.map(one_block, query_blocks).reshape(all_rows, feat_here, model_width)
    return output_proj(attended_rows, column_block, weights[7])


def feed_forward(value_rows, gain, w_in, w_out):
    model_width = value_rows.shape[-1]
    normed = normalize(value_rows, gain)
    hidden = jnp.dot(normed.reshape(-1, model_width), w_in, preferred_element_type=jnp.float32)
    activated = jax.nn.gelu(hidden).astype(jnp.bfloat16)
    result = value_rows.astype(jnp.float32) + jnp.dot(
        activated, w_out, preferred_element_type=jnp.float32
    ).reshape(value_rows.shape)
    return result.astype(jnp.bfloat16)


def local(
    table_cells,
    attn_weights,
    hidden_up_weight,
    hidden_down_weight,
    norm_gains,
    train_count,
    feature_count,
):
    weights, w_in, w_out = (
        lax.all_gather(attn_weights, "fsdp", axis=1, tiled=True),
        lax.all_gather(hidden_up_weight, "fsdp", axis=0, tiled=True),
        lax.all_gather(hidden_down_weight, "fsdp", axis=0, tiled=True),
    )
    feat_live = jnp.arange(table_cells.shape[1]) < feature_count[0]
    normed_one = normalize(table_cells, norm_gains[0])
    mixed_rows = feature_attention(table_cells, normed_one, weights, feat_live)
    fsdp_size = lax.axis_size("fsdp")
    groups = lax.axis_size("feat")
    row_dev, feat_total, model_width = table_cells.shape
    devices_all = fsdp_size * groups
    all_rows = row_dev * devices_all
    train_limit = train_count[0]
    row_index = jnp.arange(all_rows)
    split_cells = mixed_rows.reshape(row_dev, devices_all, feat_total // devices_all, model_width)
    column_block = lax.all_to_all(
        split_cells, ("fsdp", "feat"), split_axis=1, concat_axis=0, tiled=True
    )
    rows_here, single, feat_here, width_here = column_block.shape
    owner_column_block = column_block.reshape(rows_here, feat_here, width_here)
    normed_two = normalize(owner_column_block, norm_gains[1])
    sampled = sample_attention(owner_column_block, normed_two, weights, row_index < train_limit)
    at_owners = sampled.reshape(rows_here, single, feat_here, width_here)
    returned = lax.all_to_all(at_owners, ("fsdp", "feat"), split_axis=0, concat_axis=1, tiled=True)
    returned = returned.reshape(row_dev, feat_total, model_width)
    returned = feed_forward(returned, norm_gains[2], w_in, w_out)
    return returned


def solution(mesh):
    in_specs = (
        P(("fsdp", "feat"), None, None),
        P(None, "fsdp", None),
        P("fsdp", None),
        P("fsdp", None),
        P(),
        P(),
        P(),
    )
    out_specs = P(("fsdp", "feat"), None, None)
    return jax.shard_map(local, mesh=mesh, in_specs=in_specs, out_specs=out_specs, check_vma=False)
```

profile of v0, /device:TPU:1, one launch (start us, length us, event | category | flops | bytes accessed | tf_op | source)
XLA Modules:
  0.0 370.8 jit_solution(5374347418670035218)
XLA Ops:
  0.0 27.7 %all_gather.9 = bf16[8,192,192]{2,0,1:T(8,128)(2,1)S(1)} all-gather(bf16[8,6,192]{2,0,1:T(8,128)(2,1)} %param.10), channel_id=1, replica_groups=mesh['fsdp'=32,'feat'=4] {'fsdp'}, dimensions={1}, use_global_device_ids=true | all-gather | bytes 608256 | tf_op jit(solution)/shard_map/all_gather | solution.py:123
  40.0 2.8 reshape.232
  44.0 3.1 fusion.413
  47.1 3.9 %fusion.417 = (f32[12,256]{1,0:T(8,128)S(1)}, f32[12,256,256]{1,2,0:T(8,128)}) fusion(pred[256]{0:T(512)(128)(4,1)S(1)} %iota_compare_fusion.1, bf16[12,256,32]{1,0,2:T(8,128)(2,1)} %get-tuple-element.136, bf16[12,256,32]{1,0,2:T(8,128)(2,1)} %get-tuple-element.106), kind=kOutput, calls=%fused_computation.353 | convolution fusion | flops 53477632 | bytes 3551488 | tf_op jit(solution)/shard_map/sub | solution.py:22
  51.0 4.0 %fusion.426 = (f32[12,256]{1,0:T(8,128)S(1)}, f32[12,256,256]{1,2,0:T(8,128)}) fusion(pred[256]{0:T(512)(128)(4,1)S(1)} %iota_compare_fusion.1, bf16[12,256,32]{1,0,2:T(8,128)(2,1)} %get-tuple-element.137, bf16[12,256,32]{1,0,2:T(8,128)(2,1)} %get-tuple-element.105), kind=kOutput, calls=%fused_computation.354 | convolution fusion | flops 53477632 | bytes 3551488 | tf_op jit(solution)/shard_map/sub | solution.py:22
  55.0 4.0 %fusion.435 = (f32[12,256]{1,0:T(8,128)S(1)}, f32[12,256,256]{1,2,0:T(8,128)}) fusion(pred[256]{0:T(512)(128)(4,1)S(1)} %iota_compare_fusion.1, bf16[12,256,32]{1,0,2:T(8,128)(2,1)} %get-tuple-element.138, bf16[12,256,32]{1,0,2:T(8,128)(2,1)} %get-tuple-element.104), kind=kOutput, calls=%fused_computation.355 | convolution fusion | flops 53477632 | bytes 3551488 | tf_op jit(solution)/shard_map/sub | solution.py:22
  59.0 2.9 fusion.444
  61.8 2.9 fusion.453
  64.7 2.9 fusion.462
  84.9 7.2 %all-to-all-start = ((bf16[12,128,2,192]{3,2,0,1:T(2,128)(2,1)}), bf16[12,128,2,192]{3,2,0,1:T(2,128)(2,1)S(1)}, u32[]{:S(2)}, u32[]{:S(2)}) async-start(bf16[12,128,2,192]{3,2,0,1:T(2,128)(2,1)} %copy.182), calls=%async_computation | async-start | bytes 3145728 | tf_op jit(solution)/shard_map/all_to_all | solution.py:138
  92.9 24.1 %all-to-all-done = bf16[12,128,2,192]{3,2,0,1:T(2,128)(2,1)S(1)} async-done(((bf16[12,128,2,192]{3,2,0,1:T(2,128)(2,1)}), bf16[12,128,2,192]{3,2,0,1:T(2,128)(2,1)S(1)}, u32[]{:S(2)}, u32[]{:S(2)}) %all-to-all-start) | async-done | bytes 1179680 | tf_op jit(solution)/shard_map/all_to_all | solution.py:138
  118.9 4.0 %multiply_reduce_fusion.1 = f32[128,12,2]{2,1,0:T(8,128)S(1)} fusion(bf16[12,128,2,192]{3,2,0,1:T(2,128)(2,1)S(1)} %all-to-all-done, f32[128,12,2]{2,1,0:T(8,128)S(1)} %broadcast_multiply_fusion.1), kind=kLoop, calls=%fused_computation.190 | loop fusion | flops 2356224 | bytes 1204224 | tf_op jit(solution)/shard_map/reduce_sum | solution.py:15
  123.1 3.9 %multiply_convert_fusion.1 = bf16[128,12,1,2,192]{4,3,1,0,2:T(2,128)(2,1)S(1)} fusion(bf16[12,128,2,192]{3,2,0,1:T(2,128)(2,1)S(1)} %all-to-all-done, f32[192]{0:T(256)S(1)} %bitcast.148, f32[128,12,2]{2,1,0:T(8,128)S(1)} %add_rsqrt_fusion.1, f32[128,12,2]{2,1,0:T(8,128)S(1)} %broadcast_multiply_fusion.1), kind=kLoop, calls=%fused_computation.189 | loop fusion | flops 2949120 | bytes 2384640 | tf_op jit(solution)/shard_map/convert_element_type | solution.py:16
  134.0 4.9 %copy.190 = bf16[1536,2,192]{0,2,1:T(8,128)(2,1)} copy(bf16[1536,2,192]{2,1,0:T(2,128)(2,1)} %reshape.234) | data formatting | bytes 2359296
  144.4 4.9 %copy.191 = bf16[1536,2,192]{0,2,1:T(8,128)(2,1)} copy(bf16[1536,2,192]{2,1,0:T(2,128)(2,1)} %reshape.235) | data formatting | bytes 2359296
  152.6 105.7 %while.11 = (s32[]{:T(128)}, bf16[3,512,2,192]{1,3,2,0:T(8,128)(2,1)}, bf16[3,512,2,192]{1,3,2,0:T(8,128)(2,1)S(1)}, bf16[1536,2,192]{0,2,1:T(8,128)(2,1)}, bf16...) while((s32[]{:T(128)}, bf16[3,512,2,192]{1,3,2,0:T(8,128)(2,1)}, ...), condition=%wide.region_29.30_spmd.clone, body=%wide.region_16.29_spmd.clone.sunk | while | flops 1897096704 | bytes 11085937 | solution.py:98
  153.5 3.1 fusion.553
  156.7 3.3 fusion.554
  162.1 3.3 fusion.556
  167.5 3.3 fusion.558
  172.9 3.3 fusion.560
  178.4 3.3 fusion.562
  183.8 3.3 fusion.564
  188.6 3.1 fusion.553
  191.7 3.3 fusion.554
  197.1 3.3 fusion.556
  202.6 3.3 fusion.558
  208.0 3.3 fusion.560
  213.4 3.3 fusion.562
  218.9 3.3 fusion.564
  223.6 3.1 fusion.553
  226.8 3.3 fusion.554
  232.2 3.3 fusion.556
  237.6 3.3 fusion.558
  243.0 3.3 fusion.560
  248.5 3.3 fusion.562
  253.9 3.3 fusion.564
  262.0 3.3 copy.194
  265.3 2.5 fusion.223
  267.8 2.9 copy.195
  270.7 3.9 %all-to-all-start.1 = ((bf16[1536,1,2,192]{3,2,1,0:T(2,128)(2,1)}), bf16[1536,1,2,192]{3,2,1,0:T(2,128)(2,1)S(1)}, u32[]{:S(2)}, u32[]{:S(2)}) async-start(bf16[1536,1,2,192]{3,2,1,0:T(2,128)(2,1)} %copy.195), calls=%async_computation.1 | async-start | bytes 3145728 | tf_op jit(solution)/shard_map/all_to_all | solution.py:146
  274.6 39.1 %all-gather.1 = bf16[32,12,192]{2,1,0:T(8,128)(2,1)S(1)} all-gather(bf16[1,12,192]{2,1,0:T(8,128)(2,1)S(1)} %bitcast.145), channel_id=1, replica_groups=mesh['fsdp'=32,'feat'=4] {'fsdp'}, dimensions={0}, use_global_device_ids=true | all-gather | bytes 152064 | tf_op jit(solution)/shard_map/all_gather | solution.py:125
  313.8 22.8 %all-gather = bf16[32,6,384]{2,1,0:T(8,128)(2,1)S(1)} all-gather(bf16[1,6,384]{2,1,0:T(8,128)(2,1)S(1)} %bitcast.146), channel_id=1, replica_groups=mesh['fsdp'=32,'feat'=4] {'fsdp'}, dimensions={0}, use_global_device_ids=true | all-gather | bytes 152064 | tf_op jit(solution)/shard_map/all_gather | solution.py:124
  339.6 5.1 %multiply_reduce_fusion = f32[12,128,2]{2,0,1:T(8,128)} fusion(bf16[128,12,1,2,192]{4,3,1,0,2:T(2,128)(2,1)S(1)} %bitcast.137, f32[12,128,2]{2,0,1:T(8,128)S(1)} %broadcast_multiply_fusion), kind=kLoop, calls=%fused_computation.188 | loop fusion | flops 2356224 | bytes 1204224 | tf_op jit(solution)/shard_map/reduce_sum | solution.py:15
  347.3 3.4 reshape.240
  350.8 3.4 reshape.239
  362.0 5.6 %fusion.235 = f32[3072,192]{0,1:T(8,128)} fusion(bf16[384,192]{1,0:T(8,128)(2,1)S(1)} %reshape.249, bf16[192,384]{1,0:T(8,128)(2,1)S(1)} %reshape.247, f32[3072,192]{1,0:T(8,128)} %reshape.240, f32[192]{0:T(256)S(1)} %bitcast.149, f32[3072]{0:T(1024)S(1)} %rsqrt.30, f32[3072]{0:T(1024)S(1)} %div.133), kind=kOutput, calls=%fused_computation.226 | convolution fusion | flops 918945792 | bytes 5038848 | tf_op jit(solution)/shard_map/dot_general | solution.py:107
  367.6 2.9 fusion.234
  (135 shorter events, 102.2 us)
Async XLA Ops:
  0.0 29.8 %copy-start.18 = (f32[3,192]{1,0:T(4,128)S(1)}, f32[3,192]{1,0:T(4,128)}, u32[]{:S(2)}) copy-start(f32[3,192]{1,0:T(4,128)} %param.13) | copy-start | bytes 6916
  0.0 30.4 %copy-start.2 = (bf16[12,256,192]{1,2,0:T(8,128)(2,1)S(1)}, bf16[12,256,192]{1,2,0:T(8,128)(2,1)}, u32[]{:S(2)}) copy-start(bf16[12,256,192]{1,2,0:T(8,128)(2,1)} %param.9) | copy-start | bytes 3538948
  40.0 3.8 %copy-start.7 = (bf16[1,192,192]{2,0,1:T(2,128)(2,1)S(1)}, bf16[1,192,192]{2,0,1:T(2,128)(2,1)}, u32[]{:S(2)}) copy-start(bf16[1,192,192]{2,0,1:T(2,128)(2,1)} %get-tuple-element.118) | copy-start | bytes 221188
  64.7 2.9 copy-start.15
  67.6 2.4 copy-start.14
  67.6 2.9 copy-start.24
  70.6 0.9 copy-start.13
  70.6 2.0 copy-start.23
  72.6 0.9 copy-start.12
  72.6 2.0 copy-start.22
  74.5 1.9 copy-start.21
  76.4 1.9 copy-start.20
  82.6 9.4 %copy-start.6 = (bf16[1,192,192]{2,0,1:T(2,128)(2,1)S(1)}, bf16[1,192,192]{2,0,1:T(2,128)(2,1)}, u32[]{:S(2)}) copy-start(bf16[1,192,192]{2,0,1:T(2,128)(2,1)} %get-tuple-element.113) | copy-start | bytes 221188
  84.9 32.1 %all-to-all-start = ((bf16[12,128,2,192]{3,2,0,1:T(2,128)(2,1)}), bf16[12,128,2,192]{3,2,0,1:T(2,128)(2,1)S(1)}, u32[]{:S(2)}, u32[]{:S(2)}) async-start(bf16[12,128,2,192]{3,2,0,1:T(2,128)(2,1)} %copy.182), calls=%async_computation | async-start | bytes 3145728 | tf_op jit(solution)/shard_map/all_to_all | solution.py:138
  117.0 6.0 %copy-start = (bf16[12,128,2,192]{3,2,0,1:T(2,128)(2,1)}, bf16[12,128,2,192]{3,2,0,1:T(2,128)(2,1)S(1)}, u32[]{:S(2)}) copy-start(bf16[12,128,2,192]{3,2,0,1:T(2,128)(2,1)S(1)} %all-to-all-done) | copy-start | bytes 3538948
  123.1 5.4 %copy-start.10 = (bf16[1,192,192]{2,0,1:T(2,128)(2,1)S(1)}, bf16[1,192,192]{2,0,1:T(2,128)(2,1)}, u32[]{:S(2)}) copy-start(bf16[1,192,192]{2,0,1:T(2,128)(2,1)} %get-tuple-element.120) | copy-start | bytes 221188
  131.9 7.1 %copy-start.9 = (bf16[1,192,192]{2,0,1:T(2,128)(2,1)S(1)}, bf16[1,192,192]{2,0,1:T(2,128)(2,1)}, u32[]{:S(2)}) copy-start(bf16[1,192,192]{2,0,1:T(2,128)(2,1)} %get-tuple-element.119) | copy-start | bytes 221188
  142.3 7.0 %copy-start.8 = (bf16[1,192,192]{2,0,1:T(2,128)(2,1)S(1)}, bf16[1,192,192]{2,0,1:T(2,128)(2,1)}, u32[]{:S(2)}) copy-start(bf16[1,192,192]{2,0,1:T(2,128)(2,1)} %get-tuple-element.114) | copy-start | bytes 221188
  153.5 3.1 copy-start.5
  188.6 3.1 copy-start.5
  223.6 3.1 copy-start.5
  258.4 2.5 copy-start.1
  261.9 3.4 copy-start.11
  267.8 6.8 %copy-start.16 = (bf16[12,192]{1,0:T(8,128)(2,1)S(1)}, bf16[12,192]{1,0:T(8,128)(2,1)}, u32[]{:S(2)}) copy-start(bf16[12,192]{1,0:T(8,128)(2,1)} %param.12) | copy-start | bytes 13828
  267.8 46.0 %copy-start.17 = (bf16[6,384]{1,0:T(8,128)(2,1)S(1)}, bf16[6,384]{1,0:T(8,128)(2,1)}, u32[]{:S(2)}) copy-start(bf16[6,384]{1,0:T(8,128)(2,1)} %param.11) | copy-start | bytes 13828
  270.7 66.0 %all-to-all-start.1 = ((bf16[1536,1,2,192]{3,2,1,0:T(2,128)(2,1)}), bf16[1536,1,2,192]{3,2,1,0:T(2,128)(2,1)S(1)}, u32[]{:S(2)}, u32[]{:S(2)}) async-start(bf16[1536,1,2,192]{3,2,1,0:T(2,128)(2,1)} %copy.195), calls=%async_computation.1 | async-start | bytes 3145728 | tf_op jit(solution)/shard_map/all_to_all | solution.py:146
  354.2 5.6 %copy-start.3 = (f32[12,256,192]{2,1,0:T(8,128)S(1)}, f32[12,256,192]{2,1,0:T(8,128)}, u32[]{:S(2)}) copy-start(f32[12,256,192]{2,1,0:T(8,128)} %reshape.239) | copy-start | bytes 7077892
  358.3 3.7 copy-start.19
  362.0 5.6 %copy-start.4 = (f32[12,256,192]{1,2,0:T(8,128)S(1)}, f32[12,256,192]{1,2,0:T(8,128)}, u32[]{:S(2)}) copy-start(f32[12,256,192]{1,2,0:T(8,128)} %copy.203) | copy-start | bytes 7077892
where the time goes:
time: 378 us; the launch traced here: 371 us
  matrix products  143 us (38%)
  blocking collectives  89.6 us (24%)
  local copies, waits for them, and re-layouts  74.2 us (20%)
  other arithmetic  26.4 us (7%)
  waiting for transfers between devices  24.1 us (6%)
  starting transfers between devices  11 us (3%)
    sub x24, matrix products, softmax_rows(): exponent = jnp.exp(masked - row_maximum)  62.1 us
    dot_general x18, matrix products, one_block(): jnp.einsum('tdj,jtn->dtn', attention_probabilities, value_rows[..., train...  59.2 us
    all_gather x1, blocking collectives, local(): lax.all_gather(hidden_down_weight, 'fsdp', axis=0, tiled=True)  39.1 us
    all_gather x1, blocking collectives, local(): lax.all_gather(attn_weights, 'fsdp', axis=1, tiled=True)  27.7 us
    all_to_all x1, waiting for transfers between devices, local(): lax.all_to_all(split_cells, ('fsdp', 'feat'), split_axis=1, concat_axis=0...  24.1 us
    all_gather x1, blocking collectives, local(): lax.all_gather(hidden_up_weight, 'fsdp', axis=0, tiled=True)  22.8 us
    unnamed x55, local copies, waits for them, and re-layouts  18.9 us
    reshape x5, local copies, waits for them, and re-layouts, project(): product.astype(jnp.bfloat16).reshape(normed.shape[:-1] + (weight.shape[1],))  10.6 us
  transfers between devices with their start and end apart: 2, of which 1 were waited for; matrix products, arithmetic and copies ran while one was open for 0% of the time, Pallas kernels for 0%

commit v1 on v0

--- a/solution.py
+++ b/solution.py
@@ -135,8 +135,14 @@
     train_limit = train_count[0]
     row_index = jnp.arange(all_rows)
     split_cells = mixed_rows.reshape(row_dev, devices_all, feat_total // devices_all, model_width)
-    column_block = lax.all_to_all(
-        split_cells, ("fsdp", "feat"), split_axis=1, concat_axis=0, tiled=True
+    column_block = jnp.concatenate(
+        lax.all_to_all(
+            jnp.stack(jnp.split(split_cells, lax.axis_size(("fsdp", "feat")), axis=1), axis=0),
+            ("fsdp", "feat"),
+            0,
+            0,
+        ),
+        axis=0,
     )
     rows_here, single, feat_here, width_here = column_block.shape
     owner_column_block = column_block.reshape(rows_here, feat_here, width_here)

time: 378 us -> 468 us (1.24)
  local copies, waits for them, and re-layouts: 74.2 us -> 150 us
  loops' own time: 0.67 us -> 17.7 us
    unnamed x55 -> x182, local copies, waits for them, and re-layouts: 18.9 us -> 96.4 us
    another operation x1, loops' own time: 0.67 us -> 17.7 us  [sample_attention(): lax.map(one_block, query_blocks).reshape(all_rows, feat_here, model_width)]
where the time goes in v1:
time: 468 us; the launch traced here: 462 us
  local copies, waits for them, and re-layouts  150 us (32%)
  matrix products  143 us (31%)
  blocking collectives  89.5 us (19%)
  other arithmetic  25.1 us (5%)
  waiting for transfers between devices  24.1 us (5%)
  loops' own time  17.7 us (4%)
  starting transfers between devices  11.2 us (2%)
    unnamed x182, local copies, waits for them, and re-layouts  96.4 us
    sub x24, matrix products, softmax_rows(): exponent = jnp.exp(masked - row_maximum)  62.1 us
    dot_general x18, matrix products, one_block(): jnp.einsum('tdj,jtn->dtn', attention_probabilities, value_rows[..., train...  59.2 us
    all_gather x1, blocking collectives, local(): lax.all_gather(hidden_down_weight, 'fsdp', axis=0, tiled=True)  39.2 us
    all_gather x1, blocking collectives, local(): lax.all_gather(attn_weights, 'fsdp', axis=1, tiled=True)  27.5 us
    all_to_all x1, waiting for transfers between devices, local(): lax.all_to_all(jnp.stack(jnp.split(split_cells, lax.axis_size(('fsdp', 'f...  24.1 us
    all_gather x1, blocking collectives, local(): lax.all_gather(hidden_up_weight, 'fsdp', axis=0, tiled=True)  22.8 us
    another operation x1, loops' own time, sample_attention(): lax.map(one_block, query_blocks).reshape(all_rows, feat_here, model_width)  17.7 us
  transfers between devices with their start and end apart: 2, of which 1 were waited for; matrix products, arithmetic and copies ran while one was open for 0% of the time, Pallas kernels for 0%

profile of v1, /device:TPU:1, one launch (start us, length us, event | category | flops | bytes accessed | tf_op | source)
XLA Modules:
  0.0 461.6 jit_solution(2638384497584270838)
XLA Ops:
  0.0 27.5 %all_gather.9 = bf16[8,192,192]{2,0,1:T(8,128)(2,1)S(1)} all-gather(bf16[8,6,192]{2,0,1:T(8,128)(2,1)} %param.10), channel_id=1, replica_groups=mesh['fsdp'=32,'feat'=4] {'fsdp'}, dimensions={1}, use_global_device_ids=true | all-gather | bytes 608256 | tf_op jit(solution)/shard_map/all_gather | solution.py:123
  37.5 2.5 convolution_convert_fusion.3
  39.9 2.8 reshape.226
  43.9 3.1 fusion.413
  46.9 3.9 fusion.417
  50.9 4.0 fusion.426
  54.8 4.0 fusion.435
  58.8 2.9 fusion.444
  61.7 2.9 fusion.453
  64.6 2.9 fusion.462
  160.8 7.2 %all-to-all-start = ((bf16[128,12,1,2,192]{4,3,1,2,0:T(2,128)(2,1)}), bf16[128,12,1,2,192]{4,3,1,2,0:T(2,128)(2,1)S(1)}, u32[]{:S(2)}, u32[]{:S(2)}) async-start(bf16[128,12,1,2,192]{4,3,1,2,0:T(2,128)(2,1)} %constant_dynamic-update-slice_fusion), calls=%async_computation | async-start | bytes 3145728 | tf_op jit(solution)/shard_map/all_to_all | solution.py:139
  168.8 24.1 %all-to-all-done = bf16[128,12,1,2,192]{4,3,1,2,0:T(2,128)(2,1)S(1)} async-done(((bf16[128,12,1,2,192]{4,3,1,2,0:T(2,128)(2,1)}), bf16[128,12,1,2,192]{4,3,1,2,0:T(2,128)(2,1)S(1)}, u32[]{:S(2)}, u32[]{:S(2)}) %all-to-all-start) | async-done | bytes 1179680 | tf_op jit(solution)/shard_map/all_to_all | solution.py:139
  194.8 4.0 multiply_reduce_fusion.1
  199.0 3.9 multiply_convert_fusion.1
  210.0 4.9 %copy.816 = bf16[1536,2,192]{0,2,1:T(8,128)(2,1)} copy(bf16[1536,2,192]{2,1,0:T(2,128)(2,1)} %reshape.228) | data formatting | bytes 2359296
  220.4 4.9 %copy.817 = bf16[1536,2,192]{0,2,1:T(8,128)(2,1)} copy(bf16[1536,2,192]{2,1,0:T(2,128)(2,1)} %reshape.229) | data formatting | bytes 2359296
  228.6 122.8 %while.11 = (s32[]{:T(128)}, bf16[3,512,2,192]{1,3,2,0:T(8,128)(2,1)}, bf16[3,512,2,192]{1,3,2,0:T(8,128)(2,1)S(1)}, bf16[1536,2,192]{0,2,1:T(8,128)(2,1)}, bf16...) while((s32[]{:T(128)}, bf16[3,512,2,192]{1,3,2,0:T(8,128)(2,1)}, ...), condition=%wide.region_29.30_spmd.clone, body=%wide.region_16.29_spmd.clone.sunk | while | flops 1897096704 | bytes 11085937 | solution.py:98
  246.6 3.1 fusion.553
  249.8 3.3 fusion.554
  255.2 3.3 fusion.556
  260.6 3.3 fusion.558
  266.0 3.3 fusion.560
  271.5 3.3 fusion.562
  276.9 3.3 fusion.564
  281.7 3.1 fusion.553
  284.8 3.3 fusion.554
  290.2 3.3 fusion.556
  295.7 3.3 fusion.558
  301.1 3.3 fusion.560
  306.5 3.3 fusion.562
  311.9 3.3 fusion.564
  316.7 3.1 fusion.553
  319.8 3.3 fusion.554
  325.3 3.3 fusion.556
  330.7 3.3 fusion.558
  336.1 3.3 fusion.560
  341.6 3.3 fusion.562
  347.0 3.3 fusion.564
  353.2 3.2 copy.820
  358.5 2.9 copy.821
  361.4 4.0 all-to-all-start.1
  365.4 39.2 %all-gather.1 = bf16[32,12,192]{2,1,0:T(8,128)(2,1)S(1)} all-gather(bf16[1,12,192]{2,1,0:T(8,128)(2,1)S(1)} %bitcast.896), channel_id=1, replica_groups=mesh['fsdp'=32,'feat'=4] {'fsdp'}, dimensions={0}, use_global_device_ids=true | all-gather | bytes 152064 | tf_op jit(solution)/shard_map/all_gather | solution.py:125
  404.7 22.8 %all-gather = bf16[32,6,384]{2,1,0:T(8,128)(2,1)S(1)} all-gather(bf16[1,6,384]{2,1,0:T(8,128)(2,1)S(1)} %bitcast.897), channel_id=1, replica_groups=mesh['fsdp'=32,'feat'=4] {'fsdp'}, dimensions={0}, use_global_device_ids=true | all-gather | bytes 152064 | tf_op jit(solution)/shard_map/all_gather | solution.py:124
  430.4 5.1 %multiply_reduce_fusion = f32[12,128,2]{2,0,1:T(8,128)} fusion(bf16[128,12,1,2,192]{4,3,1,0,2:T(2,128)(2,1)S(1)} %bitcast.889, f32[12,128,2]{2,0,1:T(8,128)S(1)} %broadcast_multiply_fusion), kind=kLoop, calls=%fused_computation.186 | loop fusion | flops 2356224 | bytes 1204224 | tf_op jit(solution)/shard_map/reduce_sum | solution.py:15
  438.2 3.4 reshape.234
  441.6 3.4 reshape.233
  452.8 5.6 %fusion.235 = f32[3072,192]{0,1:T(8,128)} fusion(bf16[384,192]{1,0:T(8,128)(2,1)S(1)} %reshape.241, bf16[192,384]{1,0:T(8,128)(2,1)S(1)} %reshape.239, f32[3072,192]{1,0:T(8,128)} %reshape.234, f32[192]{0:T(256)S(1)} %bitcast.900, f32[3072]{0:T(1024)S(1)} %rsqrt.30, f32[3072]{0:T(1024)S(1)} %div.133), kind=kOutput, calls=%fused_computation.225 | convolution fusion | flops 918945792 | bytes 5038848 | tf_op jit(solution)/shard_map/dot_general | solution.py:107
  458.4 2.9 fusion.234
  (261 shorter events, 176.0 us)
Async XLA Ops:
  27.5 2.2 copy-start.18
  27.5 2.7 copy-start.2
  42.7 1.0 copy-start.7
  64.6 2.9 copy-start.15
  67.5 2.4 copy-start.14
  67.5 2.9 copy-start.24
  70.4 0.9 copy-start.13
  70.4 2.0 copy-start.23
  72.4 0.9 copy-start.12
  72.4 2.0 copy-start.22
  74.4 1.9 copy-start.21
  76.3 1.9 copy-start.20
  160.8 7.2 %copy-start.6 = (bf16[1,192,192]{2,0,1:T(2,128)(2,1)S(1)}, bf16[1,192,192]{2,0,1:T(2,128)(2,1)}, u32[]{:S(2)}) copy-start(bf16[1,192,192]{2,0,1:T(2,128)(2,1)} %get-tuple-element.113) | copy-start | bytes 221188
  160.8 32.1 %all-to-all-start = ((bf16[128,12,1,2,192]{4,3,1,2,0:T(2,128)(2,1)}), bf16[128,12,1,2,192]{4,3,1,2,0:T(2,128)(2,1)S(1)}, u32[]{:S(2)}, u32[]{:S(2)}) async-start(bf16[128,12,1,2,192]{4,3,1,2,0:T(2,128)(2,1)} %constant_dynamic-update-slice_fusion), calls=%async_computation | async-start | bytes 3145728 | tf_op jit(solution)/shard_map/all_to_all | solution.py:139
  193.0 6.0 %copy-start = (bf16[128,12,1,2,192]{4,3,1,2,0:T(2,128)(2,1)}, bf16[128,12,1,2,192]{4,3,1,2,0:T(2,128)(2,1)S(1)}, u32[]{:S(2)}) copy-start(bf16[128,12,1,2,192]{4,3,1,2,0:T(2,128)(2,1)S(1)} %all-to-all-done) | copy-start | bytes 3538948
  202.9 1.5 copy-start.10
  210.0 4.9 %copy-start.9 = (bf16[1,192,192]{2,0,1:T(2,128)(2,1)S(1)}, bf16[1,192,192]{2,0,1:T(2,128)(2,1)}, u32[]{:S(2)}) copy-start(bf16[1,192,192]{2,0,1:T(2,128)(2,1)} %get-tuple-element.119) | copy-start | bytes 221188
  220.4 4.9 %copy-start.8 = (bf16[1,192,192]{2,0,1:T(2,128)(2,1)S(1)}, bf16[1,192,192]{2,0,1:T(2,128)(2,1)}, u32[]{:S(2)}) copy-start(bf16[1,192,192]{2,0,1:T(2,128)(2,1)} %get-tuple-element.114) | copy-start | bytes 221188
  246.6 3.1 copy-start.5
  281.7 3.1 copy-start.5
  316.7 3.1 copy-start.5
  351.5 1.8 copy-start.1
  353.2 3.2 copy-start.11
  361.4 4.0 copy-start.16
  361.4 43.3 %copy-start.17 = (bf16[6,384]{1,0:T(8,128)(2,1)S(1)}, bf16[6,384]{1,0:T(8,128)(2,1)}, u32[]{:S(2)}) copy-start(bf16[6,384]{1,0:T(8,128)(2,1)} %param.11) | copy-start | bytes 13828
  361.4 66.1 %all-to-all-start.1 = ((bf16[1536,1,2,192]{3,2,1,0:T(2,128)(2,1)}), bf16[1536,1,2,192]{3,2,1,0:T(2,128)(2,1)S(1)}, u32[]{:S(2)}, u32[]{:S(2)}) async-start(bf16[1536,1,2,192]{3,2,1,0:T(2,128)(2,1)} %copy.821), calls=%async_computation.1 | async-start | bytes 3145728 | tf_op jit(solution)/shard_map/all_to_all | solution.py:152
  446.4 4.2 copy-start.3
  450.6 2.2 copy-start.19
  452.8 5.6 %copy-start.4 = (f32[12,256,192]{1,2,0:T(8,128)S(1)}, f32[12,256,192]{1,2,0:T(8,128)}, u32[]{:S(2)}) copy-start(f32[12,256,192]{1,2,0:T(8,128)} %copy.829) | copy-start | bytes 7077892
